TPU v7x, 128 devices: a whole 4x4x4 slice. The times are simulated.
128 devices in a mesh: row: 8 (over z_hi, y), col: 16 (over z_lo, x, core).
Axes of the slice: x: 4, y: 4, z: 4 (z_hi: 2, z_lo: 2; z = z_hi * 2 + z_lo), core: 2. Of those that a mesh axis runs over, the one named last changes fastest.
Arguments:
- tokens: bfloat16 [1024, 16384], P('col', 'row'), may hold values from -6 to 6
- dropout_keep_mask: int32 [1024, 16384], P('col', 'row'), may hold values 0 or 1
- frozen_gate_weight: bfloat16 [16384, 16384], P('row', 'col'), may hold values from -0.046875 to 0.046875
- frozen_up_weight: bfloat16 [16384, 16384], P('row', 'col'), may hold values from -0.046875 to 0.046875
- down_weight: bfloat16 [16384, 16384], P('col', 'row'), may hold values from -0.046875 to 0.046875
- adapter_input_maps: bfloat16 [32, 16384], P(None, 'row'), may hold values from -0.046875 to 0.046875
- adapter_output_maps: bfloat16 [2, 16, 16384], P(None, None, 'col'), may hold values from -1.5 to 1.5
- out_grad: bfloat16 [1024, 16384], P('col', 'row'), may hold values from -6 to 6
Outputs:
- mixed_out: bfloat16 [1024, 16384], P('col', 'row')
- token_input_gradient: bfloat16 [1024, 16384], P('col', 'row')
- grad_adapt_in: float32 [32, 16384], P(None, 'row')
- adapter_output_gradient: float32 [2, 16, 16384], P(None, None, 'col')
All inputs are finite; a program needn't handle non-finite values. No bound on the sum of `dropout_keep_mask` on one device may be relied on, other than what follows from the above.
Results may differ from a plain program's by a relative error of at most 0.033.
Values may be sent and summed in bfloat16 or wider, within the bound.
No kernel may reach another device: no remote copies, remote signals or barrier semaphores. Data moves between devices by JAX's collectives and lax.ppermute only.
A program may use at most 128 MiB of HBM per device.

v0:
```python
import jax
import jax.numpy as jnp
from jax import lax
from jax.sharding import PartitionSpec as P

keep_scale = 10.0 / 9.0
adapter_scale = 0.5


def matmul_left_transposed(left, right):
    return lax.dot_general(
        left, right, (((0,), (0,)), ((), ())), preferred_element_type=jnp.float32
    )


def matmul_right_transposed(left, right):
    return lax.dot_general(
        left, right, (((1,), (1,)), ((), ())), preferred_element_type=jnp.float32
    )


def local(
    tokens,
    dropout_keep_mask,
    frozen_gate_weight,
    frozen_up_weight,
    down_weight,
    adapter_input_maps,
    adapter_output_maps,
    out_grad,
):
    row_index = lax.axis_index("row")
    col_index = lax.axis_index("col")
    col_tokens = tokens.shape[0]
    all_tokens = col_tokens * lax.axis_size("col")
    row_tokens = all_tokens // lax.axis_size("row")
    hidden_feature_width = frozen_gate_weight.shape[1]
    adapter_rank = adapter_output_maps.shape[1]
    dropped = tokens * dropout_keep_mask.astype(jnp.bfloat16)
    low_part = matmul_right_transposed(dropped, adapter_input_maps)
    low_local = (lax.psum(low_part, "row") * keep_scale).astype(jnp.bfloat16)
    low_all = lax.all_gather(low_local, "col", axis=0, tiled=True)
    block_rows = lax.all_gather(tokens, "col", axis=0, tiled=True)
    partial_gu = jnp.concatenate(
        [
            jnp.dot(block_rows, frozen_gate_weight, preferred_element_type=jnp.float32),
            jnp.dot(block_rows, frozen_up_weight, preferred_element_type=jnp.float32),
        ],
        axis=1,
    )
    summed_product = lax.psum_scatter(
        partial_gu.astype(jnp.bfloat16), "row", scatter_dimension=0, tiled=True
    ).astype(jnp.float32)
    low_used = lax.dynamic_slice_in_dim(low_all, row_index * row_tokens, row_tokens, 0)
    gate_activation = summed_product[:, :hidden_feature_width] + adapter_scale * jnp.dot(
        low_used[:, :adapter_rank], adapter_output_maps[0], preferred_element_type=jnp.float32
    )
    up_activation = summed_product[:, hidden_feature_width:] + adapter_scale * jnp.dot(
        low_used[:, adapter_rank:], adapter_output_maps[1], preferred_element_type=jnp.float32
    )
    sigmoid_gate = jax.nn.sigmoid(gate_activation)
    activated = gate_activation * sigmoid_gate
    hidden = (activated * up_activation).astype(jnp.bfloat16)
    partial_out = jnp.dot(
        lax.all_gather(hidden, "row", axis=0, tiled=True),
        down_weight,
        preferred_element_type=jnp.float32,
    )
    mixed_out = lax.psum_scatter(
        partial_out.astype(jnp.bfloat16), "col", scatter_dimension=0, tiled=True
    )
    partial_dh = matmul_right_transposed(
        lax.all_gather(out_grad, "col", axis=0, tiled=True), down_weight
    )
    hidden_grad = lax.psum_scatter(
        partial_dh.astype(jnp.bfloat16), "row", scatter_dimension=0, tiled=True
    ).astype(jnp.float32)
    gate_gradient = (
        hidden_grad * up_activation * sigmoid_gate * (1.0 + gate_activation * (1.0 - sigmoid_gate))
    ).astype(jnp.bfloat16)
    up_gradient = (hidden_grad * activated).astype(jnp.bfloat16)
    reduced_gradient_part = adapter_scale * jnp.concatenate(
        [
            matmul_right_transposed(gate_gradient, adapter_output_maps[0]),
            matmul_right_transposed(up_gradient, adapter_output_maps[1]),
        ],
        axis=1,
    )
    outer_product_terms = adapter_scale * jnp.stack(
        [
            matmul_left_transposed(low_used[:, :adapter_rank], gate_gradient),
            matmul_left_transposed(low_used[:, adapter_rank:], up_gradient),
        ]
    )
    adapter_output_gradient = lax.psum(outer_product_terms.astype(jnp.bfloat16), "row").astype(
        jnp.float32
    )
    reduced_gradient = lax.psum(reduced_gradient_part, "col")
    scaled_product = (reduced_gradient * keep_scale).astype(jnp.bfloat16)
    scaled_all = lax.all_gather(scaled_product, "row", axis=0, tiled=True)
    scaled_own = lax.dynamic_slice_in_dim(scaled_all, col_index * col_tokens, col_tokens, 0)
    joined = jnp.concatenate([gate_gradient, up_gradient], axis=1)
    block_rows = lax.all_gather(joined, "row", axis=0, tiled=True)
    partial_dx = matmul_right_transposed(
        block_rows[:, :hidden_feature_width], frozen_gate_weight
    ) + matmul_right_transposed(block_rows[:, hidden_feature_width:], frozen_up_weight)
    adapter_output_part = dropout_keep_mask.astype(jnp.float32) * jnp.dot(
        scaled_own, adapter_input_maps, preferred_element_type=jnp.float32
    )
    token_input_gradient = (
        lax.psum_scatter(
            partial_dx.astype(jnp.bfloat16), "col", scatter_dimension=0, tiled=True
        ).astype(jnp.float32)
        + adapter_output_part
    ).astype(jnp.bfloat16)
    grad_adapt_in = lax.psum(
        matmul_left_transposed(scaled_own, dropped).astype(jnp.bfloat16), "col"
    ).astype(jnp.float32)
    return (mixed_out, token_input_gradient, grad_adapt_in, adapter_output_gradient)


def solution(mesh):
    placed = (
        P("col", "row"),
        P("col", "row"),
        P("row", "col"),
        P("row", "col"),
        P("col", "row"),
        P(None, "row"),
        P(None, None, "col"),
        P("col", "row"),
    )
    return jax.shard_map(
        local,
        mesh=mesh,
        in_specs=placed,
        out_specs=(P("col", "row"), P("col", "row"), P(None, "row"), P(None, None, "col")),
        check_vma=False,
    )
```

profile of v0, /device:TPU:30, one launch (start us, length us, event | category | flops | bytes accessed | tf_op | source)
XLA Modules:
  0.0 727.3 jit_solution(7373889922529047536)
XLA Ops:
  7.2 0.7 all-gather.6.cloned.1.call-update
  8.0 0.7 all-gather.10.cloned.1.call-update
  8.7 0.0 reduce-scatter.13.cloned.1.call-start
  8.7 39.8 %all-gather.6.cloned.1.call-done = bf16[1024,2048]{1,0:T(8,128)(2,1)} async-done(((bf16[64,2048]{1,0:T(8,128)(2,1)}), bf16[1024,2048]{1,0:T(8,128)(2,1)}) %all-gather.6.cloned.1.call-update) | async-done | bytes 4194320 | tf_op jit(solution)/shard_map/all_gather | solution.py:43
  48.5 8.2 %convolution_convert_fusion.3 = bf16[1024,1024]{0,1:T(8,128)(2,1)S(1)} fusion(bf16[1024,2048]{1,0:T(8,128)(2,1)} %all-gather.6.cloned.1.call-done, bf16[2048,1024]{1,0:T(8,128)(2,1)} %param.11), kind=kOutput, calls=%fused_computation.11 | convolution fusion | flops 4296015872 | bytes 10485760 | tf_op jit(solution)/shard_map/dot_general | solution.py:47
  56.7 4.8 convolution_convert_fusion.4
  61.5 2.4 pad_maximum_fusion
  63.9 6.6 copy.23
  70.5 0.0 reduce-scatter.15.cloned.1.call-start
  70.6 17.1 %all-gather.10.cloned.1.call-done = bf16[1024,2048]{1,0:T(8,128)(2,1)} async-done(((bf16[64,2048]{1,0:T(8,128)(2,1)}), bf16[1024,2048]{1,0:T(8,128)(2,1)}) %all-gather.10.cloned.1.call-update) | async-done | bytes 4194320 | tf_op jit(solution)/shard_map/all_gather | solution.py:73
  87.7 9.4 %convolution_convert_fusion.2 = bf16[1024,1024]{1,0:T(8,128)(2,1)} fusion(bf16[1024,2048]{1,0:T(8,128)(2,1)} %all-gather.10.cloned.1.call-done, bf16[1024,2048]{1,0:T(8,128)(2,1)} %param.12), kind=kOutput, calls=%fused_computation.10 | convolution fusion | flops 4296015872 | bytes 10485760 | tf_op jit(solution)/shard_map/dot_general | solution.py:17
  97.1 0.0 all-gather.12.cloned.1.call-start
  97.1 0.2 fusion.34
  97.3 36.6 %psum.28 = f32[64,32]{0,1:T(8,128)S(1)} all-reduce(f32[64,32]{0,1:T(8,128)S(1)} %fusion.34), channel_id=1, replica_groups=mesh['row'=8,'col'=16] {'row'}, use_global_device_ids=true, to_apply=%region_1.0 | all-reduce | flops 2048 | bytes 16384 | tf_op jit(solution)/shard_map/psum | solution.py:41
  133.9 16.7 %all-gather = bf16[16,64,32]{1,2,0:T(8,128)(2,1)S(1)} all-gather(bf16[1,64,32]{1,2,0:T(8,128)(2,1)S(1)} %fusion.23), channel_id=1, replica_groups=mesh['row'=8,'col'=16] {'col'}, dimensions={0}, use_global_device_ids=true | all-gather | bytes 69632 | tf_op jit(solution)/shard_map/all_gather | solution.py:42
  150.6 0.1 copy.20
  150.7 0.1 reshape.9
  150.8 26.4 %reduce-scatter.13.cloned.1.call-done = bf16[128,2048]{1,0:T(8,128)(2,1)} async-done(((bf16[1024,2048]{1,0:T(8,128)(2,1)}), bf16[128,2048]{1,0:T(8,128)(2,1)}) %reduce-scatter.13.cloned.1.call-update) | async-done | bytes 524304 | tf_op jit(solution)/shard_map/reduce_scatter | solution.py:51
  177.2 1.1 convert_element_type.55
  178.4 0.3 fusion.5
  178.6 76.4 %reduce-scatter.15.cloned.1.call-done = bf16[128,1024]{1,0:T(8,128)(2,1)} async-done(((bf16[1024,1024]{1,0:T(8,128)(2,1)}), bf16[128,1024]{1,0:T(8,128)(2,1)}) %reduce-scatter.15.cloned.1.call-update) | async-done | bytes 262160 | tf_op jit(solution)/shard_map/reduce_scatter | solution.py:75
  255.0 2.1 fusion.9
  257.1 0.8 pad_maximum_fusion.1
  258.0 0.0 all-gather.8.cloned.1.call-start
  258.0 0.5 all-gather.8.cloned.1.call-update
  258.5 0.0 all-reduce.5.cloned.1.call-start
  258.6 0.2 fusion.16
  258.8 0.2 fusion.13
  259.0 50.0 %psum.29 = f32[128,32]{0,1:T(8,128)S(1)} all-reduce(f32[128,32]{0,1:T(8,128)S(1)} %maximum_multiply_fusion.1), channel_id=1, replica_groups=mesh['row'=8,'col'=16] {'col'}, use_global_device_ids=true, to_apply=%region_5.0 | all-reduce | flops 4096 | bytes 32768 | tf_op jit(solution)/shard_map/psum | solution.py:98
  308.9 28.3 %all_gather.23 = bf16[1024,32]{0,1:T(8,128)(2,1)S(1)} all-gather(bf16[128,32]{0,1:T(8,128)(2,1)S(1)} %multiply_convert_fusion.1), channel_id=1, replica_groups=mesh['row'=8,'col'=16] {'row'}, dimensions={0}, use_global_device_ids=true | all-gather | bytes 73728 | tf_op jit(solution)/shard_map/all_gather | solution.py:100
  337.2 0.1 convolution_bitcast_fusion
  337.4 0.1 convolution_bitcast_fusion.1
  337.5 0.6 fusion.12
  338.2 0.0 all-reduce.3.cloned.1.call-start
  338.2 0.9 convolution_convert_fusion.1
  339.1 0.0 reduce-scatter.11.cloned.1.call-start
  339.2 10.8 %fusion.3 = f32[1024,2048]{1,0:T(8,128)} fusion(bf16[2048,1024]{1,0:T(8,128)(2,1)} %param.10, bf16[1024,2048]{1,0:T(8,128)(2,1)} %all-gather.12.cloned.1.call-done), kind=kOutput, calls=%fused_computation.8 | convolution fusion | flops 4294967296 | bytes 14680064 | tf_op jit(solution)/shard_map/dot_general | solution.py:17
  350.1 8.4 %add_convert_fusion = bf16[1024,2048]{1,0:T(8,128)(2,1)} fusion(f32[1024,2048]{1,0:T(8,128)} %fusion.3, bf16[2048,1024]{1,0:T(8,128)(2,1)S(1)} %copy-done.5, bf16[1024,2048]{1,0:T(8,128)(2,1)S(1)} %copy-done.6), kind=kOutput, calls=%fused_computation | convolution fusion | flops 4299161600 | bytes 18874368 | tf_op jit(solution)/shard_map/dot_general | solution.py:17
  358.5 0.0 reduce-scatter.9.cloned.1.call-start
  358.5 25.5 %all-gather.8.cloned.1.call-done = bf16[1024,1024]{1,0:T(8,128)(2,1)} async-done(((bf16[128,1024]{1,0:T(8,128)(2,1)}), bf16[1024,1024]{1,0:T(8,128)(2,1)}) %all-gather.8.cloned.1.call-update) | async-done | bytes 2097168 | tf_op jit(solution)/shard_map/all_gather | solution.py:65
  384.0 9.3 %convolution_convert_fusion = bf16[1024,2048]{1,0:T(8,128)(2,1)} fusion(bf16[1024,1024]{1,0:T(8,128)(2,1)} %all-gather.8.cloned.1.call-done, bf16[1024,2048]{1,0:T(8,128)(2,1)} %param.12), kind=kOutput, calls=%fused_computation.2 | convolution fusion | flops 4297064448 | bytes 10485760 | tf_op jit(solution)/shard_map/dot_general | solution.py:64
  393.3 74.1 %all-reduce.5.cloned.1.call-done = bf16[2,16,1024]{2,1,0:T(8,128)(2,1)} async-done(((bf16[2,16,1024]{2,1,0:T(8,128)(2,1)}), bf16[2,16,1024]{2,1,0:T(8,128)(2,1)}) %all-reduce.5.cloned.1.call-update) | async-done | bytes 65552 | tf_op jit(solution)/shard_map/psum | solution.py:95
  467.5 1.5 convert_element_type.72
  469.0 114.5 %all-reduce.3.cloned.1.call-done = bf16[32,2048]{1,0:T(8,128)(2,1)} async-done(((bf16[32,2048]{1,0:T(8,128)(2,1)}), bf16[32,2048]{1,0:T(8,128)(2,1)}) %all-reduce.3.cloned.1.call-update) | async-done | bytes 131088 | tf_op jit(solution)/shard_map/psum | solution.py:116
  583.5 1.6 convert_element_type.70
  585.1 67.1 %reduce-scatter.11.cloned.1.call-done = bf16[64,2048]{1,0:T(8,128)(2,1)} async-done(((bf16[1024,2048]{1,0:T(8,128)(2,1)}), bf16[64,2048]{1,0:T(8,128)(2,1)}) %reduce-scatter.11.cloned.1.call-update) | async-done | bytes 262160 | tf_op jit(solution)/shard_map/reduce_scatter | solution.py:111
  652.2 2.0 fusion.1
  654.2 66.3 %reduce-scatter.9.cloned.1.call-done = bf16[64,2048]{1,0:T(8,128)(2,1)} async-done(((bf16[1024,2048]{1,0:T(8,128)(2,1)}), bf16[64,2048]{1,0:T(8,128)(2,1)}) %reduce-scatter.9.cloned.1.call-update) | async-done | bytes 262160 | tf_op jit(solution)/shard_map/reduce_scatter | solution.py:69
  (29 shorter events, 0.3 us)
Async XLA Ops:
  7.2 90.0 %copy-start = (bf16[32,2048]{1,0:T(8,128)(2,1)S(1)}, bf16[32,2048]{1,0:T(8,128)(2,1)}, u32[]{:S(2)}) copy-start(bf16[32,2048]{1,0:T(8,128)(2,1)} %param.13) | copy-start | bytes 393220
  7.2 41.3 %all-gather.6.cloned.1.call-start = ((), (), s32[]{:S(2)}) async-start(), calls=%async_computation.4 | async-start | bytes 4456448 | tf_op jit(solution)/shard_map/all_gather | solution.py:43
  7.9 79.8 %all-gather.10.cloned.1.call-start = ((), (), s32[]{:S(2)}) async-start(), calls=%async_computation.7 | async-start | bytes 4456448 | tf_op jit(solution)/shard_map/all_gather | solution.py:73
  8.7 168.5 %reduce-scatter.13.cloned.1.call-start = ((), (), s32[]{:S(2)}) async-start(), calls=%async_computation.12 | async-start | bytes 4718592 | tf_op jit(solution)/shard_map/reduce_scatter | solution.py:51
  48.5 8.2 %copy-start.4 = (bf16[2048,1024]{1,0:T(8,128)(2,1)S(1)}, bf16[2048,1024]{1,0:T(8,128)(2,1)}, u32[]{:S(2)}) copy-start(bf16[2048,1024]{1,0:T(8,128)(2,1)} %param.10) | copy-start | bytes 12582916
  48.5 8.2 %copy-start.7 = (bf16[1024,2048]{1,0:T(8,128)(2,1)S(1)}, bf16[1024,2048]{1,0:T(8,128)(2,1)}, u32[]{:S(2)}) copy-start(bf16[1024,2048]{1,0:T(8,128)(2,1)} %all-gather.6.cloned.1.call-done) | copy-start | bytes 12582916
  70.5 26.6 %copy-start.1 = (s32[64,2048]{1,0:T(8,128)S(1)}, s32[64,2048]{1,0:T(8,128)}, u32[]{:S(2)}) copy-start(s32[64,2048]{1,0:T(8,128)} %param.9) | copy-start | bytes 1572868
  70.5 26.6 %copy-start.2 = (bf16[64,2048]{1,0:T(8,128)(2,1)S(1)}, bf16[64,2048]{1,0:T(8,128)(2,1)}, u32[]{:S(2)}) copy-start(bf16[64,2048]{1,0:T(8,128)(2,1)} %param.8) | copy-start | bytes 786436
  70.5 184.5 %reduce-scatter.15.cloned.1.call-start = ((), (), s32[]{:S(2)}) async-start(), calls=%async_computation.13 | async-start | bytes 2359296 | tf_op jit(solution)/shard_map/reduce_scatter | solution.py:75
  97.0 81.3 %copy-start.3 = (bf16[2,16,1024]{2,1,0:T(8,128)(2,1)S(1)}, bf16[2,16,1024]{2,1,0:T(8,128)(2,1)}, u32[]{:S(2)}) copy-start(bf16[2,16,1024]{2,1,0:T(8,128)(2,1)} %param.14) | copy-start | bytes 196612
  97.1 242.2 %all-gather.12.cloned.1.call-start = ((), (), s32[]{:S(2)}) async-start(), calls=%async_computation.8 | async-start | bytes 4718592 | tf_op jit(solution)/shard_map/all_gather | solution.py:103
  258.0 126.1 %all-gather.8.cloned.1.call-start = ((), (), s32[]{:S(2)}) async-start(), calls=%async_computation.5 | async-start | bytes 2359296 | tf_op jit(solution)/shard_map/all_gather | solution.py:65
  258.5 208.9 %all-reduce.5.cloned.1.call-start = ((), (), s32[]{:S(2)}) async-start(), calls=%async_computation.11 | async-start | bytes 131072 | tf_op jit(solution)/shard_map/psum | solution.py:95
  338.2 245.3 %all-reduce.3.cloned.1.call-start = ((), (), s32[]{:S(2)}) async-start(), calls=%async_computation.10 | async-start | bytes 262144 | tf_op jit(solution)/shard_map/psum | solution.py:116
  339.1 313.1 %reduce-scatter.11.cloned.1.call-start = ((), (), s32[]{:S(2)}) async-start(), calls=%async_computation.9 | async-start | bytes 4456448 | tf_op jit(solution)/shard_map/reduce_scatter | solution.py:111
  339.2 10.8 %copy-start.5 = (bf16[2048,1024]{1,0:T(8,128)(2,1)S(1)}, bf16[2048,1024]{1,0:T(8,128)(2,1)}, u32[]{:S(2)}) copy-start(bf16[2048,1024]{1,0:T(8,128)(2,1)} %param.11) | copy-start | bytes 12582916
  339.2 10.8 %copy-start.6 = (bf16[1024,2048]{1,0:T(8,128)(2,1)S(1)}, bf16[1024,2048]{1,0:T(8,128)(2,1)}, u32[]{:S(2)}) copy-start(bf16[1024,2048]{1,0:T(8,128)(2,1)} %all-gather.12.cloned.1.call-done) | copy-start | bytes 12582916
  358.5 362.0 %reduce-scatter.9.cloned.1.call-start = ((), (), s32[]{:S(2)}) async-start(), calls=%async_computation.6 | async-start | bytes 4456448 | tf_op jit(solution)/shard_map/reduce_scatter | solution.py:69
Sparse Core Ops, SparseCore 0:
  9.7 38.7 all-gather.5
  50.2 37.4 all-gather.9
  91.5 85.6 reduce-scatter.12
  180.8 74.1 reduce-scatter.14
  258.1 69.1 all-gather.11
  330.3 53.6 all-gather.7
  387.2 80.2 all-reduce.4
  470.5 112.9 all-reduce.2
  586.0 66.1 reduce-scatter.10
  655.2 65.2 reduce-scatter.8
where the time goes:
time: 732 us; the launch traced here: 727 us
  waiting for transfers between devices  509 us (70%)
  blocking collectives  132 us (18%)
  matrix products  56.9 us (8%)
  between operations  14.3 us (2%)
  other arithmetic  8.15 us (1%)
    psum x1, waiting for transfers between devices, local(): lax.psum(matmul_left_transposed(scaled_own, dropped).astype(jnp.bfloat16)...  114 us
    reduce_scatter x1, waiting for transfers between devices, local(): lax.psum_scatter(partial_dh.astype(jnp.bfloat16), 'row', scatter_dimensio...  76.4 us
    psum x1, waiting for transfers between devices, local(): lax.psum(outer_product_terms.astype(jnp.bfloat16), 'row')  74.1 us
    reduce_scatter x1, waiting for transfers between devices, local(): lax.psum_scatter(partial_dx.astype(jnp.bfloat16), 'col', scatter_dimensio...  67.1 us
    reduce_scatter x1, waiting for transfers between devices, local(): lax.psum_scatter(partial_out.astype(jnp.bfloat16), 'col', scatter_dimensi...  66.3 us
    psum x1, blocking collectives, local(): reduced_gradient = lax.psum(reduced_gradient_part, 'col')  50 us
    all_gather x1, waiting for transfers between devices, local(): block_rows = lax.all_gather(tokens, 'col', axis=0, tiled=True)  39.8 us
    psum x1, blocking collectives, local(): low_local = (lax.psum(low_part, 'row') * keep_scale).astype(jnp.bfloat16)  36.6 us
  transfers between devices with their start and end apart: 10, of which 9 were waited for; matrix products, arithmetic and copies ran while one was open for 9% of the time, Pallas kernels for 0%

commit v1 on v0

v1 whole, which is shorter than its diff:
```python
import jax
import jax.numpy as jnp
from jax import lax
from jax.sharding import Mesh
from jax.sharding import PartitionSpec as P

keep_scale = 10.0 / 9.0
adapter_scale = 0.5

ROW = ("zh", "y")
COL = ("zl", "x", "c")
CHIPS = ("zl", "x")


def dot_f32(left, right):
    return jnp.dot(left, right, preferred_element_type=jnp.float32)


def dot_left_t(left, right):
    return lax.dot_general(
        left, right, (((0,), (0,)), ((), ())), preferred_element_type=jnp.float32
    )


def dot_right_t(left, right):
    return lax.dot_general(
        left, right, (((1,), (1,)), ((), ())), preferred_element_type=jnp.float32
    )


def after(value, *others):
    return lax.optimization_barrier((value, *others))[0]


def exchange(blocks, axes):
    return lax.all_to_all(blocks, axes, 0, 0, tiled=True)


def spread(block, axes, count):
    return exchange(jnp.broadcast_to(block[None], (count, *block.shape)), axes)


def sum_blocks(blocks):
    return jnp.sum(blocks.astype(jnp.float32), axis=0)


def swap_core(value):
    return lax.ppermute(value, "c", [(0, 1), (1, 0)])


def local(tokens, mask, w_gate, w_up, w_down, a_in, a_out, out_grad):
    bf16, f32 = jnp.bfloat16, jnp.float32
    core = lax.axis_index("c")
    row_index = lax.axis_index(ROW)
    col_index = lax.axis_index(COL)
    rank = a_out.shape[1]
    hidden_width = w_gate.shape[1]
    col_tokens, features = tokens.shape
    n_col, n_row = lax.axis_size(COL), lax.axis_size(ROW)
    n_chips = n_col // 2
    all_tokens = col_tokens * n_col
    row_tokens = all_tokens // n_row

    tokens_all = lax.all_gather(tokens, COL, axis=0, tiled=True)
    dropped = tokens * mask.astype(bf16)
    low_part = dot_right_t(dropped, a_in)
    out_grad = after(out_grad, low_part)
    out_grad_all = lax.all_gather(out_grad, COL, axis=0, tiled=True)
    low_local = (sum_blocks(spread(low_part, ROW, n_row)) * keep_scale).astype(bf16)
    low_all = spread(low_local, COL, n_col).reshape(all_tokens, 2 * rank)
    w_in = jnp.concatenate([w_gate, w_up], axis=1)

    partial_gu = dot_f32(tokens_all, w_in).astype(bf16)
    dropped_all = lax.all_gather(after(dropped, partial_gu), COL, axis=0, tiled=True)
    gate_up = sum_blocks(exchange(partial_gu.reshape(n_row, row_tokens, 2 * hidden_width), ROW))
    partial_dh = dot_right_t(out_grad_all, w_down).astype(bf16)
    hidden_grad = sum_blocks(exchange(partial_dh.reshape(n_row, row_tokens, hidden_width), ROW))

    low_used = lax.dynamic_slice_in_dim(low_all, row_index * row_tokens, row_tokens, 0)
    gate = gate_up[:, :hidden_width] + adapter_scale * dot_f32(low_used[:, :rank], a_out[0])
    up = gate_up[:, hidden_width:] + adapter_scale * dot_f32(low_used[:, rank:], a_out[1])
    sig = jax.nn.sigmoid(gate)
    act = gate * sig
    hidden = (act * up).astype(bf16)
    gate_grad = (hidden_grad * up * sig * (1.0 + gate * (1.0 - sig))).astype(bf16)
    up_grad = (hidden_grad * act).astype(bf16)

    hidden_all = spread(hidden, ROW, n_row).reshape(all_tokens, hidden_width)
    partial_out = dot_f32(hidden_all, w_down).astype(bf16)
    mixed_out = lax.psum_scatter(partial_out, COL, scatter_dimension=0, tiled=True)

    low_grad_part = adapter_scale * jnp.concatenate(
        [dot_right_t(gate_grad, a_out[0]), dot_right_t(up_grad, a_out[1])], axis=1
    )
    scaled = (sum_blocks(spread(low_grad_part, COL, n_col)) * keep_scale).astype(bf16)
    joined = jnp.concatenate(
        [gate_grad, up_grad, jnp.pad(scaled, ((0, 0), (0, 128 - 2 * rank)))], axis=1
    )
    joined_all = spread(joined, ROW, n_row).reshape(all_tokens, 2 * hidden_width + 128)
    scaled_all = joined_all[:, 2 * hidden_width : 2 * hidden_width + 2 * rank]
    grads_all = joined_all[:, : 2 * hidden_width]

    by_core = grads_all.reshape(n_chips, 2, col_tokens, 2 * hidden_width)
    half = n_chips * col_tokens

    def input_part(which):
        rows = lax.dynamic_index_in_dim(by_core, which, 1, False).reshape(half, 2 * hidden_width)
        return dot_right_t(rows, w_in)

    away = swap_core(input_part(1 - core).astype(bf16))
    chip_sum = (input_part(core) + away.astype(f32)).astype(bf16)
    frozen_part = sum_blocks(exchange(chip_sum.reshape(n_chips, col_tokens, features), CHIPS))
    scaled_own = lax.dynamic_slice_in_dim(scaled_all, col_index * col_tokens, col_tokens, 0)
    adapter_part = mask.astype(f32) * dot_f32(scaled_own, a_in)
    token_input_gradient = (frozen_part + adapter_part).astype(bf16)

    grad_adapt_in = dot_left_t(scaled_all, dropped_all)
    adapter_output_gradient = adapter_scale * jnp.stack(
        [
            dot_left_t(low_all[:, :rank], grads_all[:, :hidden_width]),
            dot_left_t(low_all[:, rank:], grads_all[:, hidden_width:]),
        ]
    )
    return mixed_out, token_input_gradient, grad_adapt_in, adapter_output_gradient


def solution(mesh):
    split = Mesh(mesh.devices.reshape(2, 4, 2, 4, 2), (*ROW, *COL))
    both = P(COL, ROW)
    return jax.shard_map(
        local,
        mesh=split,
        in_specs=(
            both,
            both,
            P(ROW, COL),
            P(ROW, COL),
            both,
            P(None, ROW),
            P(None, None, COL),
            both,
        ),
        out_specs=(both, both, P(None, ROW), P(None, None, COL)),
        check_vma=False,
    )
```

time: 732 us -> 394 us (0.54)
  waiting for transfers between devices: 509 us -> 238 us
  blocking collectives: 132 us -> 10 us
  starting transfers between devices: 0.4 us -> 46.7 us
  local copies, waits for them, and re-layouts: 6.82 us -> 18.3 us
    reduce_scatter x4 -> x1, waiting for transfers between devices: 236 us -> 0.01 us  [local(): lax.psum_scatter(partial_out, COL, scatter_dimension=0, tiled=True)]
    psum x2 -> x0, waiting for transfers between devices: 189 us -> none  [the longest x1 114 us: local(): lax.psum(matmul_left_transposed(scaled_own, dropped).astype(jnp.bfloat16)...]
    all_to_all x0 -> x7, waiting for transfers between devices: none -> 173 us  [exchange(): return lax.all_to_all(blocks, axes, 0, 0, tiled=True)]
    psum x2 -> x0, blocking collectives: 86.6 us -> none  [the longest x1 50 us: local(): reduced_gradient = lax.psum(reduced_gradient_part, 'col')]
    all_to_all x0 -> x7, starting transfers between devices: none -> 46.6 us  [exchange(): return lax.all_to_all(blocks, axes, 0, 0, tiled=True)]
    all_gather x2 -> x0, blocking collectives: 44.9 us -> none  [the longest x1 28.3 us: local(): scaled_all = lax.all_gather(scaled_product, 'row', axis=0, tiled=True)]
    all_gather x4 -> x3, waiting for transfers between devices: 82.4 us -> 59.3 us  [the longest x1 43.4 us: local(): tokens_all = lax.all_gather(tokens, COL, axis=0, tiled=True)]
    all_to_all x0 -> x1, blocking collectives: none -> 10 us  [exchange(): return lax.all_to_all(blocks, axes, 0, 0, tiled=True)]
  transfers between devices with their start and end apart: 10 -> 12, of which waited for: 9 -> 7; matrix products, arithmetic and copies ran while one was open for 9% -> 21% of each run, Pallas kernels for 0% -> 0%
where the time goes in v1:
time: 394 us; the launch traced here: 393 us
  waiting for transfers between devices  238 us (60%)
  matrix products  58.7 us (15%)
  starting transfers between devices  46.7 us (12%)
  local copies, waits for them, and re-layouts  18.3 us (5%)
  between operations  14 us (4%)
  blocking collectives  10 us (3%)
  other arithmetic  6.54 us (2%)
    all_to_all x7, waiting for transfers between devices, exchange(): return lax.all_to_all(blocks, axes, 0, 0, tiled=True)  173 us
    all_to_all x7, starting transfers between devices, exchange(): return lax.all_to_all(blocks, axes, 0, 0, tiled=True)  46.6 us
    all_gather x1, waiting for transfers between devices, local(): tokens_all = lax.all_gather(tokens, COL, axis=0, tiled=True)  43.4 us
    dot_general x6, matrix products, dot_right_t(): lax.dot_general(left, right, (((1,), (1,)), ((), ())), preferred_element_...  27.2 us
    dot_general x5, matrix products, dot_f32(): return jnp.dot(left, right, preferred_element_type=jnp.float32)  23.7 us
    all_gather x1, waiting for transfers between devices, local(): out_grad_all = lax.all_gather(out_grad, COL, axis=0, tiled=True)  15.8 us
    all_to_all x1, blocking collectives, exchange(): return lax.all_to_all(blocks, axes, 0, 0, tiled=True)  10 us
  transfers between devices with their start and end apart: 12, of which 7 were waited for; matrix products, arithmetic and copies ran while one was open for 21% of the time, Pallas kernels for 0%

profile of v1, /device:TPU:30, one launch (start us, length us, event | category | flops | bytes accessed | tf_op | source)
XLA Modules:
  0.0 392.6 jit_solution(17859138953886409250)
XLA Ops:
  7.2 1.2 convert_multiply_fusion
  8.4 0.2 fusion.36
  8.7 0.7 all-gather.4.cloned.1.call-update
  9.4 0.8 reshape.68
  10.2 8.0 %all-to-all-start.1 = ((f32[8,1,2048]{2,1,0:T(1,128)}), f32[8,1,2048]{2,1,0:T(1,128)S(1)}, u32[]{:S(2)}, u32[]{:S(2)}) async-start(f32[8,1,2048]{2,1,0:T(1,128)} %reshape.68), calls=%async_computation.1 | async-start | bytes 131072 | tf_op jit(solution)/shard_map/all_to_all | solution.py:36
  18.2 4.8 %constant_dynamic-update-slice_fusion.1 = bf16[2048,2048]{1,0:T(8,128)(2,1)} fusion(bf16[2048,1024]{1,0:T(8,128)(2,1)} %param.10), kind=kLoop, calls=%fused_computation.48 | loop fusion | bytes 8388608
  23.0 2.5 constant_dynamic-update-slice_fusion
  25.6 0.5 broadcast.33
  26.1 0.8 reduce
  27.0 0.8 reshape.70
  27.8 5.2 %all-to-all-start.2 = ((bf16[16,2,1024]{2,1,0:T(2,128)(2,1)}), bf16[16,2,1024]{2,1,0:T(2,128)(2,1)S(1)}, u32[]{:S(2)}, u32[]{:S(2)}) async-start(bf16[16,2,1024]{2,1,0:T(2,128)(2,1)} %reshape.70), calls=%async_computation.2 | async-start | bytes 131072 | tf_op jit(solution)/shard_map/all_to_all | solution.py:36
  33.0 15.8 %all-gather.6.cloned.1.call-done = bf16[1024,2048]{1,0:T(8,128)(2,1)} async-done(((bf16[64,2048]{1,0:T(8,128)(2,1)}), bf16[1024,2048]{1,0:T(8,128)(2,1)}) %all-gather.6.cloned.1.call-update) | async-done | bytes 4194320 | tf_op jit(solution)/shard_map/all_gather | solution.py:68
  48.9 9.3 %convolution_convert_fusion.3 = bf16[1024,1024]{1,0:T(8,128)(2,1)} fusion(bf16[1024,2048]{1,0:T(8,128)(2,1)} %all-gather.6.cloned.1.call-done, bf16[1024,2048]{1,0:T(8,128)(2,1)} %param.12), kind=kOutput, calls=%fused_computation.14 | convolution fusion | flops 4296015872 | bytes 10485760 | tf_op jit(solution)/shard_map/dot_general | solution.py:26
  58.2 7.1 %all-to-all-start.4 = ((bf16[8,128,1024]{2,1,0:T(8,128)(2,1)}), bf16[8,128,1024]{2,1,0:T(8,128)(2,1)S(1)}, u32[]{:S(2)}, u32[]{:S(2)}) async-start(bf16[8,128,1024]{2,1,0:T(8,128)(2,1)} %bitcast.57), calls=%async_computation.5 | async-start | bytes 4194304 | tf_op jit(solution)/shard_map/all_to_all | solution.py:36
  65.3 43.4 %all-gather.4.cloned.1.call-done = bf16[1024,2048]{1,0:T(8,128)(2,1)} async-done(((bf16[64,2048]{1,0:T(8,128)(2,1)}), bf16[1024,2048]{1,0:T(8,128)(2,1)}) %all-gather.4.cloned.1.call-update) | async-done | bytes 4194320 | tf_op jit(solution)/shard_map/all_gather | solution.py:64
  108.7 13.8 %convolution_convert_fusion = bf16[2048,1024]{0,1:T(8,128)(2,1)} fusion(bf16[1024,2048]{1,0:T(8,128)(2,1)} %all-gather.4.cloned.1.call-done, bf16[2048,2048]{1,0:T(8,128)(2,1)} %constant_dynamic-update-slice_fusion), kind=kOutput, calls=%fused_computation.4 | convolution fusion | flops 8592031744 | bytes 16777216 | tf_op jit(solution)/shard_map/dot_general | solution.py:16
  122.5 7.3 %all-to-all-start = ((bf16[8,128,2048]{2,1,0:T(8,128)(2,1)}), bf16[8,128,2048]{2,1,0:T(8,128)(2,1)}, u32[]{:S(2)}, u32[]{:S(2)}) async-start(bf16[8,128,2048]{2,1,0:T(8,128)(2,1)} %bitcast.52), calls=%async_computation | async-start | bytes 8388608 | tf_op jit(solution)/shard_map/all_to_all | solution.py:36
  129.8 0.7 all-gather.8.cloned.1.call-update
  130.7 0.1 reshape.60
  130.9 0.3 convert_reduce_fusion.2
  131.2 60.8 %all-to-all-done = bf16[8,128,2048]{2,1,0:T(8,128)(2,1)} async-done(((bf16[8,128,2048]{2,1,0:T(8,128)(2,1)}), bf16[8,128,2048]{2,1,0:T(8,128)(2,1)}, u32[]{:S(2)}, u32[]{:S(2)}) %all-to-all-start) | async-done | bytes 4194336 | tf_op jit(solution)/shard_map/all_to_all | solution.py:36
  192.0 3.1 convert_reduce_fusion
  195.1 0.3 fusion.7
  195.4 0.5 multiply_convert_fusion.1
  195.9 0.2 fusion.19
  196.1 0.2 fusion.22
  196.3 10.0 %all_to_all.40 = f32[16,128,32]{1,2,0:T(8,128)S(1)} all-to-all(f32[16,128,32]{1,2,0:T(8,128)S(1)} %broadcast_in_dim.13), channel_id=1, replica_groups=mesh['zh'=2,'y'=4,'zl'=2,'x'=4,'c'=2] {'zl','x','c'}, dimensions={0} | all-to-all | bytes 524288 | tf_op jit(solution)/shard_map/all_to_all | solution.py:36
  206.3 1.6 broadcast_in_dim.12
  208.0 7.5 %all-to-all-start.3 = ((bf16[8,128,1024]{2,1,0:T(8,128)(2,1)}), bf16[8,128,1024]{2,1,0:T(8,128)(2,1)S(1)}, u32[]{:S(2)}, u32[]{:S(2)}) async-start(bf16[8,128,1024]{2,1,0:T(8,128)(2,1)} %broadcast_in_dim.12), calls=%async_computation.3 | async-start | bytes 4194304 | tf_op jit(solution)/shard_map/all_to_all | solution.py:36
  215.7 30.4 %all-to-all-done.3 = bf16[8,128,1024]{2,1,0:T(8,128)(2,1)S(1)} async-done(((bf16[8,128,1024]{2,1,0:T(8,128)(2,1)}), bf16[8,128,1024]{2,1,0:T(8,128)(2,1)S(1)}, u32[]{:S(2)}, u32[]{:S(2)}) %all-to-all-start.3) | async-done | bytes 2097184 | tf_op jit(solution)/shard_map/all_to_all | solution.py:36
  246.1 2.6 broadcast_in_dim.14
  248.6 6.9 %all-to-all-start.6 = ((bf16[8,128,2176]{2,1,0:T(8,128)(2,1)}), bf16[8,128,2176]{2,1,0:T(8,128)(2,1)}, u32[]{:S(2)}, u32[]{:S(2)}) async-start(bf16[8,128,2176]{2,1,0:T(8,128)(2,1)} %broadcast_in_dim.14), calls=%async_computation.7 | async-start | bytes 8912896 | tf_op jit(solution)/shard_map/all_to_all | solution.py:36
  255.6 8.3 %convolution_convert_fusion.1 = bf16[1024,2048]{1,0:T(8,128)(2,1)} fusion(bf16[1024,1024]{1,0:T(8,128)(2,1)S(1)} %bitcast.56, bf16[1024,2048]{1,0:T(8,128)(2,1)} %param.12), kind=kOutput, calls=%fused_computation.5 | convolution fusion | flops 4297064448 | bytes 10485760 | tf_op jit(solution)/shard_map/dot_general | solution.py:16
  263.9 62.6 %all-to-all-done.6 = bf16[8,128,2176]{2,1,0:T(8,128)(2,1)} async-done(((bf16[8,128,2176]{2,1,0:T(8,128)(2,1)}), bf16[8,128,2176]{2,1,0:T(8,128)(2,1)}, u32[]{:S(2)}, u32[]{:S(2)}) %all-to-all-start.6) | async-done | bytes 4456480 | tf_op jit(solution)/shard_map/all_to_all | solution.py:36
  326.5 2.5 slice.54
  329.0 0.6 constant_dynamic-slice_fusion
  329.6 8.2 %convolution_convert_fusion.2 = bf16[512,2048]{1,0:T(8,128)(2,1)S(1)} fusion(bf16[512,2048]{1,0:T(8,128)(2,1)S(1)} %bitcast.54, bf16[2048,2048]{1,0:T(8,128)(2,1)} %constant_dynamic-update-slice_fusion), kind=kOutput, calls=%fused_computation.6 | convolution fusion | flops 4296015872 | bytes 12582912 | tf_op jit(solution)/shard_map/dot_general | solution.py:26
  337.9 4.1 %collective-permute-done = bf16[512,2048]{1,0:T(8,128)(2,1)S(1)} collective-permute-done((bf16[512,2048]{1,0:T(8,128)(2,1)S(1)}, bf16[512,2048]{1,0:T(8,128)(2,1)S(1)}, u32[]{:S(2)}, u32[]{:S(2)}) %collective-permute-start) | collective-permute-done | bytes 2097184 | tf_op jit(solution)/shard_map/ppermute | solution.py:48
  342.1 9.1 %add_convert_fusion = bf16[512,2048]{1,0:T(8,128)(2,1)} fusion(bf16[512,2048]{1,0:T(8,128)(2,1)S(1)} %collective-permute-done, bf16[512,2048]{1,0:T(8,128)(2,1)S(1)} %bitcast.53, bf16[2048,2048]{1,0:T(8,128)(2,1)} %constant_dynamic-update-slice_fusion), kind=kOutput, calls=%fused_computation.2 | convolution fusion | flops 4298113024 | bytes 14680064 | tf_op jit(solution)/shard_map/dot_general | solution.py:26
  351.2 4.5 %all-to-all-start.7 = ((bf16[8,64,2048]{2,1,0:T(8,128)(2,1)}), bf16[8,64,2048]{2,1,0:T(8,128)(2,1)S(1)}, u32[]{:S(2)}, u32[]{:S(2)}) async-start(bf16[8,64,2048]{2,1,0:T(8,128)(2,1)} %bitcast.55), calls=%async_computation.8 | async-start | bytes 4194304 | tf_op jit(solution)/shard_map/all_to_all | solution.py:36
  355.7 1.0 slice.55
  356.7 2.0 fusion.11
  358.7 2.0 fusion.8
  360.7 0.7 maximum_multiply_fusion
  361.3 3.8 fusion.34
  365.2 19.6 %all-to-all-done.7 = bf16[8,64,2048]{2,1,0:T(8,128)(2,1)S(1)} async-done(((bf16[8,64,2048]{2,1,0:T(8,128)(2,1)}), bf16[8,64,2048]{2,1,0:T(8,128)(2,1)S(1)}, u32[]{:S(2)}, u32[]{:S(2)}) %all-to-all-start.7) | async-done | bytes 2097184 | tf_op jit(solution)/shard_map/all_to_all | solution.py:36
  384.8 0.3 convert_reduce_fusion.1
  385.1 0.9 fusion.1
  (35 shorter events, 0.8 us)
Async XLA Ops:
  7.2 1.3 copy-start
  7.2 41.7 %all-gather.6.cloned.1.call-start = ((), (), s32[]{:S(2)}) async-start(), calls=%async_computation.11 | async-start | bytes 4456448 | tf_op jit(solution)/shard_map/all_gather | solution.py:68
  8.4 14.6 %copy-start.2 = (bf16[64,2048]{1,0:T(8,128)(2,1)}, bf16[64,2048]{1,0:T(8,128)(2,1)S(1)}, u32[]{:S(2)}) copy-start(bf16[64,2048]{1,0:T(8,128)(2,1)S(1)} %convert_multiply_fusion) | copy-start | bytes 786436
  8.7 100.0 %all-gather.4.cloned.1.call-start = ((), (), s32[]{:S(2)}) async-start(), calls=%async_computation.9 | async-start | bytes 4456448 | tf_op jit(solution)/shard_map/all_gather | solution.py:64
  10.2 15.4 %all-to-all-start.1 = ((f32[8,1,2048]{2,1,0:T(1,128)}), f32[8,1,2048]{2,1,0:T(1,128)S(1)}, u32[]{:S(2)}, u32[]{:S(2)}) async-start(f32[8,1,2048]{2,1,0:T(1,128)} %reshape.68), calls=%async_computation.1 | async-start | bytes 131072 | tf_op jit(solution)/shard_map/all_to_all | solution.py:36
  18.2 4.8 %copy-start.1 = (bf16[2048,1024]{1,0:T(8,128)(2,1)S(1)}, bf16[2048,1024]{1,0:T(8,128)(2,1)}, u32[]{:S(2)}) copy-start(bf16[2048,1024]{1,0:T(8,128)(2,1)} %param.11) | copy-start | bytes 12582916
  27.8 30.4 %all-to-all-start.2 = ((bf16[16,2,1024]{2,1,0:T(2,128)(2,1)}), bf16[16,2,1024]{2,1,0:T(2,128)(2,1)S(1)}, u32[]{:S(2)}, u32[]{:S(2)}) async-start(bf16[16,2,1024]{2,1,0:T(2,128)(2,1)} %reshape.70), calls=%async_computation.2 | async-start | bytes 131072 | tf_op jit(solution)/shard_map/all_to_all | solution.py:36
  58.2 64.3 %all-to-all-start.4 = ((bf16[8,128,1024]{2,1,0:T(8,128)(2,1)}), bf16[8,128,1024]{2,1,0:T(8,128)(2,1)S(1)}, u32[]{:S(2)}, u32[]{:S(2)}) async-start(bf16[8,128,1024]{2,1,0:T(8,128)(2,1)} %bitcast.57), calls=%async_computation.5 | async-start | bytes 4194304 | tf_op jit(solution)/shard_map/all_to_all | solution.py:36
  122.5 69.5 %all-to-all-start = ((bf16[8,128,2048]{2,1,0:T(8,128)(2,1)}), bf16[8,128,2048]{2,1,0:T(8,128)(2,1)}, u32[]{:S(2)}, u32[]{:S(2)}) async-start(bf16[8,128,2048]{2,1,0:T(8,128)(2,1)} %bitcast.52), calls=%async_computation | async-start | bytes 8388608 | tf_op jit(solution)/shard_map/all_to_all | solution.py:36
  129.8 231.5 %all-gather.8.cloned.1.call-start = ((), (), s32[]{:S(2)}) async-start(), calls=%async_computation.12 | async-start | bytes 4456448 | tf_op jit(solution)/shard_map/all_gather | solution.py:74
  130.7 64.5 %copy-start.4 = (bf16[2,16,1024]{2,1,0:T(8,128)(2,1)S(1)}, bf16[2,16,1024]{2,1,0:T(8,128)(2,1)}, u32[]{:S(2)}) copy-start(bf16[2,16,1024]{2,1,0:T(8,128)(2,1)} %param.14) | copy-start | bytes 196612
  208.0 38.1 %all-to-all-start.3 = ((bf16[8,128,1024]{2,1,0:T(8,128)(2,1)}), bf16[8,128,1024]{2,1,0:T(8,128)(2,1)S(1)}, u32[]{:S(2)}, u32[]{:S(2)}) async-start(bf16[8,128,1024]{2,1,0:T(8,128)(2,1)} %broadcast_in_dim.12), calls=%async_computation.3 | async-start | bytes 4194304 | tf_op jit(solution)/shard_map/all_to_all | solution.py:36
  248.6 77.8 %all-to-all-start.6 = ((bf16[8,128,2176]{2,1,0:T(8,128)(2,1)}), bf16[8,128,2176]{2,1,0:T(8,128)(2,1)}, u32[]{:S(2)}, u32[]{:S(2)}) async-start(bf16[8,128,2176]{2,1,0:T(8,128)(2,1)} %broadcast_in_dim.14), calls=%async_computation.7 | async-start | bytes 8912896 | tf_op jit(solution)/shard_map/all_to_all | solution.py:36
  255.6 130.5 %reduce-scatter.2.cloned.1.call-start = ((), (), s32[]{:S(2)}) async-start(), calls=%async_computation.10 | async-start | bytes 4456448 | tf_op jit(solution)/shard_map/reduce_scatter | solution.py:90
  337.9 4.2 %collective-permute-start = (bf16[512,2048]{1,0:T(8,128)(2,1)S(1)}, bf16[512,2048]{1,0:T(8,128)(2,1)S(1)}, u32[]{:S(2)}, u32[]{:S(2)}) collective-permute-start(bf16[512,2048]{1,0:T(8,128)(2,1)S(1)} %convolution_convert_fusion.2), channel_id=1, source_target_pairs={{0,1},{1,0},{2,3},{3,2},{4,5},{5,4},{6,7},{7,6},{8,9},{9,8},{10,11... | collective-permute-start | bytes 6291464 | tf_op jit(solution)/shard_map/ppermute | solution.py:48
  351.2 33.6 %all-to-all-start.7 = ((bf16[8,64,2048]{2,1,0:T(8,128)(2,1)}), bf16[8,64,2048]{2,1,0:T(8,128)(2,1)S(1)}, u32[]{:S(2)}, u32[]{:S(2)}) async-start(bf16[8,64,2048]{2,1,0:T(8,128)(2,1)} %bitcast.55), calls=%async_computation.8 | async-start | bytes 4194304 | tf_op jit(solution)/shard_map/all_to_all | solution.py:36
  360.7 24.5 %copy-start.3 = (s32[64,2048]{1,0:T(8,128)S(1)}, s32[64,2048]{1,0:T(8,128)}, u32[]{:S(2)}) copy-start(s32[64,2048]{1,0:T(8,128)} %param.9) | copy-start | bytes 1572868
Sparse Core Ops, SparseCore 0:
  9.7 39.1 all-gather.5
  50.6 58.0 all-gather.3
  132.9 66.5 all-gather.7
  264.0 75.1 reduce-scatter.1
